TPU v7x, 32 devices: a whole 2x2x4 slice. The times are simulated.
32 devices in a mesh: groups: 2 (over y), tensor: 16 (over z, x, core).
Axes of the slice: x: 2, y: 2, z: 4, core: 2. Of those that a mesh axis runs over, the one named last changes fastest.
Arguments:
- token_ids: int32 [64], P(('groups', 'tensor')), parts along dimension 0, may hold values from 0 to 17
- return_ids: int32 [64], P(('groups', 'tensor')), parts along dimension 0, may hold values from 0 to 63
- token_table: bfloat16 [18, 8192], replicated, may hold values from -6 to 6
- return_table: bfloat16 [64, 8192], replicated, may hold values from -6 to 6
- norm_gain: float32 [8192], replicated, may hold values from 0.1 to 1.9
- gate_weight: bfloat16 [8192, 29568], P(None, 'tensor'), may hold values from -0.0625 to 0.0625
- up_weight: bfloat16 [8192, 29568], P(None, 'tensor'), may hold values from -0.0625 to 0.0625
- down_weight: bfloat16 [29568, 8192], P('tensor'), may hold values from -0.03125 to 0.03125
Outputs:
- mixed: bfloat16 [64, 8192], P(('groups', 'tensor')), parts along dimension 0
There are 2 independent parts, one for each index of `groups`. A program takes and returns all parts, laid end to end along the dimension named above; an argument that names none is the same for every part. Nothing has to cross between parts.
All inputs are finite; a program needn't handle non-finite values.
Results may differ from a plain program's by a relative error of at most 0.0064.
Values may be sent and summed in bfloat16 or wider, within the bound.
A program may use at most 192 MiB of HBM per device.

v0:
```python
import jax
import jax.numpy as jnp
from jax import lax
from jax.sharding import PartitionSpec as P


def look_up(ids, table):
    one_hot = (ids[:, None] == jnp.arange(table.shape[0], dtype=jnp.int32)[None, :]).astype(
        jnp.bfloat16
    )
    return jnp.dot(one_hot, table, preferred_element_type=jnp.float32)


def shards(
    token_ids, return_ids, token_table, return_table, norm_gain, gate_weight, up_weight, down_weight
):
    both_ids = jnp.stack([token_ids, return_ids], axis=1)
    id_piece = lax.all_gather(both_ids, "tensor", axis=0, tiled=True)
    stream = look_up(id_piece[:, 0], token_table) + look_up(id_piece[:, 1], return_table)
    scale = lax.rsqrt(jnp.mean(stream * stream, axis=1, keepdims=True) + 1e-06)
    normed = (stream * scale * norm_gain[None, :]).astype(jnp.bfloat16)
    gate = jnp.dot(normed, gate_weight, preferred_element_type=jnp.float32)
    up_value = jnp.dot(normed, up_weight, preferred_element_type=jnp.float32)
    hidden = (jax.nn.silu(gate) * up_value).astype(jnp.bfloat16)
    return lax.psum_scatter(
        jnp.dot(hidden, down_weight, preferred_element_type=jnp.float32),
        "tensor",
        scatter_dimension=0,
        tiled=True,
    ).astype(jnp.bfloat16)


def solution(mesh):
    in_specs = (
        P(("groups", "tensor")),
        P(("groups", "tensor")),
        P(),
        P(),
        P(),
        P(None, "tensor"),
        P(None, "tensor"),
        P("tensor", None),
    )
    out_specs = P(("groups", "tensor"), None)
    return jax.shard_map(shards, mesh=mesh, in_specs=in_specs, out_specs=out_specs, check_vma=False)
```

profile of v0, /device:TPU:0, one launch (start us, length us, event | category | flops | bytes accessed | tf_op | source)
XLA Modules:
  0.0 136.1 jit_solution(4483398836918051224)
XLA Ops:
  0.0 0.0 copy-start
  0.0 0.0 copy-start.1
  0.0 0.8 pad_add_fusion
  0.8 0.1 copy.13
  0.9 23.1 %all-gather = s32[16,2,2]{2,1,0:T(2,128)S(1)} all-gather(s32[1,2,2]{2,1,0:T(2,128)S(1)} %bitcast.13), channel_id=1, replica_groups=mesh['groups'=2,'tensor'=16] {'tensor'}, dimensions={0}, use_global_device_ids=true | all-gather | bytes 272 | tf_op jit(solution)/shard_map/all_gather | solution.py:18
  23.9 0.1 fusion.13
  24.0 0.1 copy.16
  24.1 1.3 fusion.8
  25.4 0.1 copy.17
  25.5 0.0 copy-done
  25.5 0.5 multiply_reduce_fusion
  26.0 14.6 %fusion.12 = f32[32,1848]{1,0:T(8,128)S(1)} fusion(bf16[8192,1848]{0,1:T(8,128)(2,1)} %param.13, f32[32,8192]{1,0:T(8,128)S(1)} %get-tuple-element.8, f32[8192]{0:T(1024)} %param.12, f32[32]{0:T(128)S(1)} %add_rsqrt_fusion), kind=kOutput, calls=%fused_computation.21 | convolution fusion | flops 969670656 | bytes 31595648 | tf_op jit(solution)/shard_map/dot_general | solution.py:22
  40.5 0.0 copy-done.1
  40.5 0.0 copy-start.2
  40.6 24.1 %fusion.1 = f32[32,8192]{1,0:T(8,128)S(1)} fusion(bf16[1848,8192]{1,0:T(8,128)(2,1)} %param.15, bf16[8192,1848]{0,1:T(8,128)(2,1)} %param.14, f32[32,1848]{1,0:T(8,128)S(1)} %fusion.12, f32[32,8192]{1,0:T(8,128)S(1)} %get-tuple-element.8, f32[8192]{0:T(1024)S(1)} %copy-done.1, f32[32]{0:T(128)S(1)} %add_rsqrt_fusion), kind=kOutput, calls=%fused_computation.3 | convolution fusion | flops 1938909696 | bytes 62921856 | tf_op jit(solution)/shard_map/dot_general | solution.py:26
  64.7 69.5 %all-reduce.2 = bf16[32,8192]{1,0:T(8,128)(2,1)S(1)} all-reduce(f32[32,8192]{1,0:T(8,128)S(1)} %fusion.1), channel_id=2, replica_groups=mesh['groups'=2,'tensor'=16] {'tensor'}, use_global_device_ids=true, to_apply=%region_1.2.clone | all-reduce | flops 262144 | bytes 1572864
  134.2 0.0 copy-done.2
  134.2 0.6 dynamic-slice
  135.5 0.7 dynamic-slice_convert_fusion
  (1 shorter events, 0.0 us)
Async XLA Ops:
  0.0 25.5 %copy-start = (bf16[64,8192]{1,0:T(8,128)(2,1)S(1)}, bf16[64,8192]{1,0:T(8,128)(2,1)}, u32[]{:S(2)}) copy-start(bf16[64,8192]{1,0:T(8,128)(2,1)} %param.11) | copy-start | bytes 3145732
  0.0 40.5 %copy-start.1 = (f32[8192]{0:T(1024)S(1)}, f32[8192]{0:T(1024)}, u32[]{:S(2)}) copy-start(f32[8192]{0:T(1024)} %param.12) | copy-start | bytes 98308
  40.5 93.7 %copy-start.2 = (u32[32]{0:T(128)S(1)}, u32[32]{0:T(128)}, u32[]{:S(2)}) copy-start(u32[32]{0:T(128)} %constant.17) | copy-start | bytes 388
where the time goes:
time: 136 us
  blocking collectives  92.6 us (68%)
  matrix products  40.5 us (30%)
  local copies, waits for them, and re-layouts  1.57 us (1%)
    unnamed x1, blocking collectives  69.5 us
    dot_general x1, matrix products, shards(): jnp.dot(hidden, down_weight, preferred_element_type=jnp.float32)  24.1 us
    all_gather x1, blocking collectives, shards(): id_piece = lax.all_gather(both_ids, 'tensor', axis=0, tiled=True)  23.1 us
    dot_general x1, matrix products, shards(): gate = jnp.dot(normed, gate_weight, preferred_element_type=jnp.float32)  14.6 us

commit v1 on v0

v1 whole, which is shorter than its diff:
```python
import functools

import jax
import jax.numpy as jnp
from jax import lax
from jax.experimental import pallas as pl
from jax.experimental.pallas import tpu as pltpu
from jax.sharding import PartitionSpec as P

MESH = pl.DeviceIdType.MESH
F32 = jnp.float32
BF16 = jnp.bfloat16
WIDE = 512
SLOT_BYTES = 50 * 1024 * 1024


def up_to(value, step):
    return -(-value // step) * step


def kernel(
    n,
    slots,
    tok_hbm,
    ret_hbm,
    tt_hbm,
    rt_hbm,
    gain_hbm,
    gate_hbm,
    up_hbm,
    down_hbm,
    out_ref,
    tok_s,
    ret_s,
    tt,
    rt,
    gain,
    idbuf,
    stream,
    normed,
    weights,
    acc_g,
    acc_u,
    hidden,
    part,
    crecv,
    turned,
    own,
    sbuf,
    rbuf,
    local_sem,
    w_sem,
    id_send,
    id_recv,
    core_send,
    core_recv,
    chip_send,
    chip_recv,
):
    me = lax.axis_index("tensor")
    core = lax.rem(me, 2)
    chip = lax.div(me, 2)
    partner = me + 1 - 2 * core
    chips = n // 2
    rows = tok_hbm.shape[0]
    tokens = rows * n
    half = tokens // 2
    d = gain.shape[1]
    pairs = d // WIDE
    chunk = 2 * WIDE
    chunks = d // chunk
    lanes = idbuf.shape[2]
    per = 16 // rows

    tok_copy = pltpu.make_async_copy(tok_hbm, tok_s, local_sem.at[0])
    ret_copy = pltpu.make_async_copy(ret_hbm, ret_s, local_sem.at[1])
    tt_copy = pltpu.make_async_copy(tt_hbm, tt, local_sem.at[2])
    rt_copy = pltpu.make_async_copy(rt_hbm, rt, local_sem.at[3])
    gain_copy = pltpu.make_async_copy(gain_hbm, gain, local_sem.at[4])
    tok_copy.start()
    ret_copy.start()

    barrier = pltpu.get_barrier_semaphore()

    def greet(k, carry):
        pl.semaphore_signal(
            barrier, inc=1, device_id={"tensor": lax.rem(me + k, n)}, device_id_type=MESH
        )
        return carry

    lax.fori_loop(1, n, greet, 0)
    tt_copy.start()
    rt_copy.start()
    gain_copy.start()

    def piece(ref, t, slot, which):
        at = pl.ds(pl.multiple_of(t * WIDE, WIDE), WIDE)
        return pltpu.make_async_copy(
            ref.at[:, at], weights.at[slot, which], w_sem.at[slot, which]
        )

    def start_gate_up(t):
        slot = lax.rem(t, slots)
        piece(gate_hbm, t, slot, 0).start()
        piece(up_hbm, t, slot, 1).start()

    def start_down(t):
        slot = lax.rem(t + pairs, slots)
        piece(down_hbm, 2 * t, slot, 0).start()
        piece(down_hbm, 2 * t + 1, slot, 1).start()

    for t in range(slots):
        if t < pairs:
            start_gate_up(jnp.int32(t))
        else:
            start_down(jnp.int32(t - pairs))

    tok_copy.wait()
    ret_copy.wait()
    lane = lax.broadcasted_iota(jnp.int32, (1, lanes), 1)
    place = core * half + chip * rows
    for kind, ids in ((0, tok_s), (1, ret_s)):
        row = jnp.zeros((1, lanes), jnp.int32)
        for i in range(rows):
            row = jnp.where(lane == place + i, ids[i], row)
        idbuf[n - 1, kind : kind + 1, :] = row

    pl.semaphore_wait(barrier, n - 1)

    def send_ids(k, carry):
        pltpu.make_async_remote_copy(
            src_ref=idbuf.at[n - 1],
            dst_ref=idbuf.at[k - 1],
            send_sem=id_send,
            recv_sem=id_recv,
            device_id={"tensor": lax.rem(me + k, n)},
            device_id_type=MESH,
        ).start()
        return carry

    lax.fori_loop(1, n, send_ids, 0)
    tt_copy.wait()
    rt_copy.wait()
    gain_copy.wait()
    others = idbuf.at[pl.ds(0, n - 1)]
    pltpu.make_async_copy(others, others, id_recv).wait()
    both = jnp.sum(idbuf[...], axis=0)

    def one_hot(row, size):
        key = lax.broadcasted_iota(jnp.int32, (128, lanes), 0)
        hot = jnp.where(key == jnp.broadcast_to(row, (128, lanes)), 1.0, 0.0).astype(F32)
        return jnp.transpose(hot)[:tokens, :size].astype(BF16)

    tok_hot = one_hot(both[0:1], tt.shape[0])
    ret_hot = one_hot(both[1:2], rt.shape[0])
    total = jnp.zeros((tokens, 1), F32)
    for c in range(chunks):
        at = slice(c * chunk, (c + 1) * chunk)
        value = jnp.dot(tok_hot, tt[:, at], preferred_element_type=F32) + jnp.dot(
            ret_hot, rt[:, at], preferred_element_type=F32
        )
        stream[:, at] = value
        total += jnp.sum(value * value, axis=1, keepdims=True)
    scale = lax.rsqrt(total / d + 1e-06)
    for c in range(chunks):
        at = slice(c * chunk, (c + 1) * chunk)
        normed[:, at] = (stream[:, at] * scale * gain[:, at]).astype(BF16)

    acc_g[...] = jnp.zeros_like(acc_g)
    acc_u[...] = jnp.zeros_like(acc_u)

    def gate_up(t, carry):
        slot = lax.rem(t, slots)
        x = normed[:, pl.ds(pl.multiple_of(t * WIDE, WIDE), WIDE)]
        for which, ref, acc in ((0, gate_hbm, acc_g), (1, up_hbm, acc_u)):
            piece(ref, t, slot, which).wait()
            acc[...] += lax.dot_general(
                x, weights[slot, which], (((1,), (1,)), ((), ())), preferred_element_type=F32
            )
        ahead = t + slots

        @pl.when(ahead < pairs)
        def _():
            start_gate_up(ahead)

        @pl.when(jnp.logical_and(ahead >= pairs, ahead < pairs + chunks))
        def _():
            start_down(ahead - pairs)

        return carry

    lax.fori_loop(0, pairs, gate_up, 0)
    gate = acc_g[...]
    hidden[...] = (gate / (1.0 + jnp.exp(-gate)) * acc_u[...]).astype(BF16)

    def core_copy(c):
        return pltpu.make_async_remote_copy(
            src_ref=part.at[c, 1 - core],
            dst_ref=crecv.at[c],
            send_sem=core_send.at[c],
            recv_sem=core_recv.at[c],
            device_id={"tensor": partner},
            device_id_type=MESH,
        )

    def project(c):
        slot = lax.rem(c + pairs, slots)
        for which in range(2):
            piece(down_hbm, 2 * c + which, slot, which).wait()
            value = jnp.dot(hidden[...], weights[slot, which], preferred_element_type=F32)
            at = slice(which * WIDE, (which + 1) * WIDE)
            part[c, 0, :, at] = value[:half]
            part[c, 1, :, at] = value[half:]
        core_copy(c).start()

    def spread(c):
        core_copy(c).wait_recv()
        mine = part.at[c, core]
        mine[...] += crecv[c]

        def turn(j):
            for q in range(per):
                turned[j, q * rows : (q + 1) * rows, :] = mine[
                    j * rows : (j + 1) * rows, q * 128 : (q + 1) * 128
                ]

        for j in range(chips):
            turn(j)
        own[c] = turned[chip]
        sbuf[c] = turned[...].astype(BF16)

        def send(k, carry):
            to = lax.rem(chip + k, chips)
            pltpu.make_async_remote_copy(
                src_ref=sbuf.at[c, to],
                dst_ref=rbuf.at[c, k - 1],
                send_sem=chip_send.at[c],
                recv_sem=chip_recv.at[c],
                device_id={"tensor": 2 * to + core},
                device_id_type=MESH,
            ).start()
            return carry

        lax.fori_loop(1, chips, send, 0)

    def finish(c):
        arrived = rbuf.at[c]
        pltpu.make_async_copy(arrived, arrived, chip_recv.at[c]).wait()
        total = own[c] + jnp.sum(rbuf[c].astype(F32), axis=0)
        out_ref[c] = total

    def down(c, carry):
        project(c)

        @pl.when(c >= 1)
        def _():
            spread(c - 1)

        @pl.when(c >= 4)
        def _():
            finish(c - 4)

        return carry

    lax.fori_loop(0, chunks, down, 0)
    spread(chunks - 1)
    for c in range(max(chunks - 4, 0), chunks):
        finish(c)

    pltpu.make_async_copy(others, others, id_send).wait()

    def drain(c, carry):
        core_copy(c).wait_send()
        arrived = rbuf.at[c]
        pltpu.make_async_copy(arrived, arrived, chip_send.at[c]).wait()
        return carry

    lax.fori_loop(0, chunks, drain, 0)


def shards(
    n, token_ids, return_ids, token_table, return_table, norm_gain, gate_weight, up_weight, down_weight
):
    d, f = gate_weight.shape
    rows = token_ids.shape[0]
    tokens = rows * n
    half = tokens // 2
    chips = n // 2
    chunk = 2 * WIDE
    chunks = d // chunk
    pairs = d // WIDE
    lanes = up_to(tokens, 128)
    slots = min(pairs + chunks, SLOT_BYTES // (2 * up_to(f, 16) * WIDE * 2))
    any_space = pl.BlockSpec(memory_space=pl.ANY)
    folded = pl.pallas_call(
        functools.partial(kernel, n, slots),
        out_shape=jax.ShapeDtypeStruct((chunks, 16, 128), F32),
        in_specs=[any_space] * 8,
        out_specs=pl.BlockSpec(memory_space=pltpu.VMEM),
        scratch_shapes=[
            pltpu.SMEM((rows,), jnp.int32),
            pltpu.SMEM((rows,), jnp.int32),
            pltpu.VMEM(token_table.shape, BF16),
            pltpu.VMEM(return_table.shape, BF16),
            pltpu.VMEM((1, d), F32),
            pltpu.VMEM((n, 2, lanes), jnp.int32),
            pltpu.VMEM((tokens, d), F32),
            pltpu.VMEM((tokens, d), BF16),
            pltpu.VMEM((slots, 2, f, WIDE), BF16),
            pltpu.VMEM((tokens, f), F32),
            pltpu.VMEM((tokens, f), F32),
            pltpu.VMEM((tokens, f), BF16),
            pltpu.VMEM((chunks, 2, half, chunk), F32),
            pltpu.VMEM((chunks, half, chunk), F32),
            pltpu.VMEM((chips, 16, 128), F32),
            pltpu.VMEM((chunks, 16, 128), F32),
            pltpu.VMEM((chunks, chips, 16, 128), BF16),
            pltpu.VMEM((chunks, chips - 1, 16, 128), BF16),
            pltpu.SemaphoreType.DMA((5,)),
            pltpu.SemaphoreType.DMA((slots, 2)),
            pltpu.SemaphoreType.DMA,
            pltpu.SemaphoreType.DMA,
            pltpu.SemaphoreType.DMA((chunks,)),
            pltpu.SemaphoreType.DMA((chunks,)),
            pltpu.SemaphoreType.DMA((chunks,)),
            pltpu.SemaphoreType.DMA((chunks,)),
        ],
        compiler_params=pltpu.CompilerParams(
            collective_id=0, has_side_effects=True, vmem_limit_bytes=61 * 1024 * 1024
        ),
        cost_estimate=pl.CostEstimate(
            flops=6 * tokens * d * f, bytes_accessed=6 * d * f, transcendentals=tokens * f
        ),
    )(
        token_ids,
        return_ids,
        token_table,
        return_table,
        norm_gain.reshape(1, d),
        gate_weight.T,
        up_weight.T,
        down_weight,
    )
    per = 16 // rows
    parts = folded.reshape(chunks, per, rows, 128).transpose(2, 0, 1, 3)
    return parts.reshape(rows, d).astype(BF16)


def solution(mesh):
    in_specs = (
        P(("groups", "tensor")),
        P(("groups", "tensor")),
        P(),
        P(),
        P(),
        P(None, "tensor"),
        P(None, "tensor"),
        P("tensor", None),
    )
    out_specs = P(("groups", "tensor"), None)
    return jax.shard_map(
        functools.partial(shards, mesh.shape["tensor"]),
        mesh=mesh,
        in_specs=in_specs,
        out_specs=out_specs,
        check_vma=False,
    )
```

time: 136 us -> 58.4 us (0.43)
  blocking collectives: 92.6 us -> 0 us
  Pallas kernels: 0 us -> 56.8 us
  matrix products: 40.5 us -> 0 us
  local copies, waits for them, and re-layouts: 1.57 us -> 0 us
    unnamed x1 -> x0, blocking collectives: 69.5 us -> none
    pallas_call x0 -> x1, Pallas kernels: none -> 56.8 us  [shards(): pl.pallas_call(functools.partial(kernel, n, slots), out_shape=jax.ShapeDt...]
    dot_general x4 -> x0, matrix products: 40.5 us -> none  [the longest x1 24.1 us: shards(): jnp.dot(hidden, down_weight, preferred_element_type=jnp.float32)]
    all_gather x1 -> x0, blocking collectives: 23.1 us -> none  [shards(): id_piece = lax.all_gather(both_ids, 'tensor', axis=0, tiled=True)]
    convert_element_type x0 -> x1, other arithmetic: none -> 1.46 us  [shards(): return parts.reshape(rows, d).astype(BF16)]
where the time goes in v1:
time: 58.4 us; the launch traced here: 58.2 us
  Pallas kernels  56.8 us (97%)
  other arithmetic  1.46 us (2%)
    pallas_call x1, Pallas kernels, shards(): pl.pallas_call(functools.partial(kernel, n, slots), out_shape=jax.ShapeDt...  56.8 us
    convert_element_type x1, other arithmetic, shards(): return parts.reshape(rows, d).astype(BF16)  1.46 us

profile of v1, /device:TPU:0, one launch (start us, length us, event | category | flops | bytes accessed | tf_op | source)
XLA Modules:
  0.0 58.2 jit_solution(12234363483631167416)
XLA Ops:
  0.0 56.8 %shard_map.82 = f32[8,16,128]{2,1,0:T(8,128)} custom-call(s32[2]{0:T(128)} %tok_hbm.1, s32[2]{0:T(128)} %ret_hbm.1, bf16[18,8192]{1,0:T(8,128)(2,1)} %tt_hbm.1, bf16[64,8192]{1,0:T(8,128)(2,1)} %rt_hbm.1, f32[1,8192]{1,0:T(1,128)} %bitcast.10, bf16[1848,8192]{1,0:T(8,128)(2,1)} %bitcast.8, bf16[1848,8192]{1,0:T(8,128)(2,1)} %bitcast.9, ...), custom_call_target="tpu_custom_call" | custom-call | flops 2906652672 | bytes 90832896 | tf_op jit(solution)/shard_map/pallas_call | solution.py:295
  56.8 1.5 %convert_element_type.12 = bf16[8,16,128]{2,1,0:T(8,128)(2,1)} convert(f32[8,16,128]{2,1,0:T(8,128)} %shard_map.82) | non-fusion elementwise | flops 16384 | bytes 98304 | tf_op jit(solution)/shard_map/convert_element_type | solution.py:346

commit v2 on v1

--- a/solution.py
+++ b/solution.py
@@ -10,8 +10,8 @@
 MESH = pl.DeviceIdType.MESH
 F32 = jnp.float32
 BF16 = jnp.bfloat16
-WIDE = 512
-SLOT_BYTES = 50 * 1024 * 1024
+WIDE = 2048
+SLOT_BYTES = 52 * 1024 * 1024
 
 
 def up_to(value, step):
@@ -66,11 +66,12 @@
     tokens = rows * n
     half = tokens // 2
     d = gain.shape[1]
-    pairs = d // WIDE
-    chunk = 2 * WIDE
+    blocks = d // WIDE
+    per = 16 // rows
+    chunk = per * 128
     chunks = d // chunk
+    pieces = WIDE // chunk
     lanes = idbuf.shape[2]
-    per = 16 // rows
 
     tok_copy = pltpu.make_async_copy(tok_hbm, tok_s, local_sem.at[0])
     ret_copy = pltpu.make_async_copy(ret_hbm, ret_s, local_sem.at[1])
@@ -93,27 +94,25 @@
     rt_copy.start()
     gain_copy.start()
 
-    def piece(ref, t, slot, which):
-        at = pl.ds(pl.multiple_of(t * WIDE, WIDE), WIDE)
+    def piece(ref, block, slot, which):
+        at = pl.ds(pl.multiple_of(block * WIDE + which * chunk, chunk), chunk)
         return pltpu.make_async_copy(
-            ref.at[:, at], weights.at[slot, which], w_sem.at[slot, which]
-        )
-
-    def start_gate_up(t):
-        slot = lax.rem(t, slots)
-        piece(gate_hbm, t, slot, 0).start()
-        piece(up_hbm, t, slot, 1).start()
-
-    def start_down(t):
-        slot = lax.rem(t + pairs, slots)
-        piece(down_hbm, 2 * t, slot, 0).start()
-        piece(down_hbm, 2 * t + 1, slot, 1).start()
-
-    for t in range(slots):
-        if t < pairs:
-            start_gate_up(jnp.int32(t))
+            ref.at[:, at],
+            weights.at[slot, :, pl.ds(which * chunk, chunk)],
+            w_sem.at[slot, which],
+        )
+
+    def start_block(ref, block, t):
+        for which in range(pieces):
+            piece(ref, block, lax.rem(t, slots), which).start()
+
+    def start_first(t):
+        if t < 2 * blocks:
+            start_block((gate_hbm, up_hbm)[t % 2], jnp.int32(t // 2), jnp.int32(t))
         else:
-            start_down(jnp.int32(t - pairs))
+            start_block(down_hbm, jnp.int32(t - 2 * blocks), jnp.int32(t))
+
+    start_first(0)
 
     tok_copy.wait()
     ret_copy.wait()
@@ -139,6 +138,8 @@
         return carry
 
     lax.fori_loop(1, n, send_ids, 0)
+    for t in range(1, slots):
+        start_first(t)
     tt_copy.wait()
     rt_copy.wait()
     gain_copy.wait()
@@ -169,27 +170,29 @@
     acc_g[...] = jnp.zeros_like(acc_g)
     acc_u[...] = jnp.zeros_like(acc_u)
 
-    def gate_up(t, carry):
-        slot = lax.rem(t, slots)
-        x = normed[:, pl.ds(pl.multiple_of(t * WIDE, WIDE), WIDE)]
-        for which, ref, acc in ((0, gate_hbm, acc_g), (1, up_hbm, acc_u)):
-            piece(ref, t, slot, which).wait()
+    def gate_up(block, carry):
+        x = normed[:, pl.ds(pl.multiple_of(block * WIDE, WIDE), WIDE)]
+        for kind, ref, acc in ((0, gate_hbm, acc_g), (1, up_hbm, acc_u)):
+            t = 2 * block + kind
+            slot = lax.rem(t, slots)
+            for which in range(pieces):
+                piece(ref, block, slot, which).wait()
             acc[...] += lax.dot_general(
-                x, weights[slot, which], (((1,), (1,)), ((), ())), preferred_element_type=F32
+                x, weights[slot], (((1,), (1,)), ((), ())), preferred_element_type=F32
             )
-        ahead = t + slots
-
-        @pl.when(ahead < pairs)
-        def _():
-            start_gate_up(ahead)
-
-        @pl.when(jnp.logical_and(ahead >= pairs, ahead < pairs + chunks))
-        def _():
-            start_down(ahead - pairs)
-
-        return carry
-
-    lax.fori_loop(0, pairs, gate_up, 0)
+            ahead = t + slots
+
+            @pl.when(ahead < 2 * blocks)
+            def _():
+                start_block((gate_hbm, up_hbm)[(kind + slots) % 2], lax.div(ahead, 2), ahead)
+
+            @pl.when(jnp.logical_and(ahead >= 2 * blocks, ahead < 3 * blocks))
+            def _():
+                start_block(down_hbm, ahead - 2 * blocks, ahead)
+
+        return carry
+
+    lax.fori_loop(0, blocks, gate_up, 0)
     gate = acc_g[...]
     hidden[...] = (gate / (1.0 + jnp.exp(-gate)) * acc_u[...]).astype(BF16)
 
@@ -203,14 +206,17 @@
             device_id_type=MESH,
         )
 
-    def project(c):
-        slot = lax.rem(c + pairs, slots)
-        for which in range(2):
-            piece(down_hbm, 2 * c + which, slot, which).wait()
-            value = jnp.dot(hidden[...], weights[slot, which], preferred_element_type=F32)
-            at = slice(which * WIDE, (which + 1) * WIDE)
-            part[c, 0, :, at] = value[:half]
-            part[c, 1, :, at] = value[half:]
+    def project(block, which):
+        c = block * pieces + which
+        slot = lax.rem(block + 2 * blocks, slots)
+        piece(down_hbm, block, slot, which).wait()
+        value = jnp.dot(
+            hidden[...],
+            weights[slot, :, which * chunk : (which + 1) * chunk],
+            preferred_element_type=F32,
+        )
+        part[c, 0] = value[:half]
+        part[c, 1] = value[half:]
         core_copy(c).start()
 
     def spread(c):
@@ -249,20 +255,22 @@
         total = own[c] + jnp.sum(rbuf[c].astype(F32), axis=0)
         out_ref[c] = total
 
-    def down(c, carry):
-        project(c)
-
-        @pl.when(c >= 1)
-        def _():
-            spread(c - 1)
-
-        @pl.when(c >= 4)
-        def _():
-            finish(c - 4)
-
-        return carry
-
-    lax.fori_loop(0, chunks, down, 0)
+    def down(block, carry):
+        for which in range(pieces):
+            project(block, which)
+            c = block * pieces + which
+
+            @pl.when(c >= 1)
+            def _():
+                spread(c - 1)
+
+            @pl.when(c >= 4)
+            def _():
+                finish(c - 4)
+
+        return carry
+
+    lax.fori_loop(0, blocks, down, 0)
     spread(chunks - 1)
     for c in range(max(chunks - 4, 0), chunks):
         finish(c)
@@ -286,11 +294,10 @@
     tokens = rows * n
     half = tokens // 2
     chips = n // 2
-    chunk = 2 * WIDE
+    chunk = 16 // rows * 128
     chunks = d // chunk
-    pairs = d // WIDE
     lanes = up_to(tokens, 128)
-    slots = min(pairs + chunks, SLOT_BYTES // (2 * up_to(f, 16) * WIDE * 2))
+    slots = min(3 * (d // WIDE), SLOT_BYTES // (up_to(f, 16) * WIDE * 2))
     any_space = pl.BlockSpec(memory_space=pl.ANY)
     folded = pl.pallas_call(
         functools.partial(kernel, n, slots),
@@ -306,7 +313,7 @@
             pltpu.VMEM((n, 2, lanes), jnp.int32),
             pltpu.VMEM((tokens, d), F32),
             pltpu.VMEM((tokens, d), BF16),
-            pltpu.VMEM((slots, 2, f, WIDE), BF16),
+            pltpu.VMEM((slots, f, WIDE), BF16),
             pltpu.VMEM((tokens, f), F32),
             pltpu.VMEM((tokens, f), F32),
             pltpu.VMEM((tokens, f), BF16),
@@ -317,7 +324,7 @@
             pltpu.VMEM((chunks, chips, 16, 128), BF16),
             pltpu.VMEM((chunks, chips - 1, 16, 128), BF16),
             pltpu.SemaphoreType.DMA((5,)),
-            pltpu.SemaphoreType.DMA((slots, 2)),
+            pltpu.SemaphoreType.DMA((slots, WIDE // chunk)),
             pltpu.SemaphoreType.DMA,
             pltpu.SemaphoreType.DMA,
             pltpu.SemaphoreType.DMA((chunks,)),

time: 58.4 us -> 45.9 us (0.79)
  Pallas kernels: 56.8 us -> 44.3 us
    pallas_call x1, Pallas kernels: 56.8 us -> 44.3 us  [shards(): pl.pallas_call(functools.partial(kernel, n, slots), out_shape=jax.ShapeDt...]
where the time goes in v2:
time: 45.9 us; the launch traced here: 45.7 us
  Pallas kernels  44.3 us (97%)
  other arithmetic  1.46 us (3%)
    pallas_call x1, Pallas kernels, shards(): pl.pallas_call(functools.partial(kernel, n, slots), out_shape=jax.ShapeDt...  44.3 us
    convert_element_type x1, other arithmetic, shards(): return parts.reshape(rows, d).astype(BF16)  1.46 us

profile of v2, /device:TPU:0, one launch (start us, length us, event | category | flops | bytes accessed | tf_op | source)
XLA Modules:
  0.0 45.7 jit_solution(18269935527313430088)
XLA Ops:
  0.0 44.3 %shard_map.82 = f32[8,16,128]{2,1,0:T(8,128)} custom-call(s32[2]{0:T(128)} %tok_hbm.1, s32[2]{0:T(128)} %ret_hbm.1, bf16[18,8192]{1,0:T(8,128)(2,1)} %tt_hbm.1, bf16[64,8192]{1,0:T(8,128)(2,1)} %rt_hbm.1, f32[1,8192]{1,0:T(1,128)} %bitcast.10, bf16[1848,8192]{1,0:T(8,128)(2,1)} %bitcast.8, bf16[1848,8192]{1,0:T(8,128)(2,1)} %bitcast.9, ...), custom_call_target="tpu_custom_call" | custom-call | flops 2906652672 | bytes 90832896 | tf_op jit(solution)/shard_map/pallas_call | solution.py:302
  44.3 1.5 %convert_element_type.12 = bf16[8,16,128]{2,1,0:T(8,128)(2,1)} convert(f32[8,16,128]{2,1,0:T(8,128)} %shard_map.82) | non-fusion elementwise | flops 16384 | bytes 98304 | tf_op jit(solution)/shard_map/convert_element_type | solution.py:353

commit v3 on v2

--- a/solution.py
+++ b/solution.py
@@ -10,7 +10,7 @@
 MESH = pl.DeviceIdType.MESH
 F32 = jnp.float32
 BF16 = jnp.bfloat16
-WIDE = 2048
+WIDE = 4096
 SLOT_BYTES = 52 * 1024 * 1024
 
 

time: 45.9 us -> 45.4 us (0.989)
  Pallas kernels: 44.3 us -> 43.8 us
    pallas_call x1, Pallas kernels: 44.3 us -> 43.8 us  [shards(): pl.pallas_call(functools.partial(kernel, n, slots), out_shape=jax.ShapeDt...]
where the time goes in v3:
time: 45.4 us; the launch traced here: 45.3 us
  Pallas kernels  43.8 us (96%)
  other arithmetic  1.46 us (3%)
    pallas_call x1, Pallas kernels, shards(): pl.pallas_call(functools.partial(kernel, n, slots), out_shape=jax.ShapeDt...  43.8 us
    convert_element_type x1, other arithmetic, shards(): return parts.reshape(rows, d).astype(BF16)  1.46 us

profile of v3, /device:TPU:0, one launch (start us, length us, event | category | flops | bytes accessed | tf_op | source)
XLA Modules:
  0.0 45.3 jit_solution(16065520542714910354)
XLA Ops:
  0.0 43.8 %shard_map.82 = f32[8,16,128]{2,1,0:T(8,128)} custom-call(s32[2]{0:T(128)} %tok_hbm.1, s32[2]{0:T(128)} %ret_hbm.1, bf16[18,8192]{1,0:T(8,128)(2,1)} %tt_hbm.1, bf16[64,8192]{1,0:T(8,128)(2,1)} %rt_hbm.1, f32[1,8192]{1,0:T(1,128)} %bitcast.10, bf16[1848,8192]{1,0:T(8,128)(2,1)} %bitcast.8, bf16[1848,8192]{1,0:T(8,128)(2,1)} %bitcast.9, ...), custom_call_target="tpu_custom_call" | custom-call | flops 2906652672 | bytes 90832896 | tf_op jit(solution)/shard_map/pallas_call | solution.py:302
  43.8 1.5 %convert_element_type.12 = bf16[8,16,128]{2,1,0:T(8,128)(2,1)} convert(f32[8,16,128]{2,1,0:T(8,128)} %shard_map.82) | non-fusion elementwise | flops 16384 | bytes 98304 | tf_op jit(solution)/shard_map/convert_element_type | solution.py:353
